TPU v7x, 256 devices: a whole 4x4x8 slice. The times are simulated.
256 devices in a mesh: ctx: 128 (over z, y, x), rsp: 2 (over core).
Axes of the slice: x: 4, y: 4, z: 8, core: 2. Of those that a mesh axis runs over, the one named last changes fastest.
Arguments:
- prompt_keys: bfloat16 [32768, 1024], P(('ctx', 'rsp')), may hold values from -3 to 3
- prompt_values: bfloat16 [32768, 1024], P(('ctx', 'rsp')), may hold values from -3 to 3
- block_offsets: int32 [128], replicated, may hold values from 0 to 127, each once
- prompt_queries: bfloat16 [32768, 8192], P(('ctx', 'rsp')), may hold values from -3 to 3
- prompt_cotangent: bfloat16 [32768, 8192], P(('ctx', 'rsp')), may hold values from -1.1953125 to 1.1953125
- prompt_lse: float32 [32768, 64], P(('ctx', 'rsp')), may hold values from 3 to 5
- prompt_delta: float32 [32768, 64], P(('ctx', 'rsp')), may hold values from -4 to 4
- response_queries: bfloat16 [16384, 8192], P(('ctx', 'rsp')), may hold values from -3 to 3
- response_cotangent: bfloat16 [16384, 8192], P(('ctx', 'rsp')), may hold values from -1.1953125 to 1.1953125
- response_lse: float32 [16384, 64], P(('ctx', 'rsp')), may hold values from 3 to 5
- response_delta: float32 [16384, 64], P(('ctx', 'rsp')), may hold values from -4 to 4
- response_ids: int32 [16384], P(('ctx', 'rsp')), may hold values from 0 to 15
- advantages: float32 [16], replicated, may hold values from -4 to 4
Outputs:
- response_grad: bfloat16 [16384, 8192], P(('ctx', 'rsp'))
- prompt_grad: bfloat16 [32768, 8192], P(('ctx', 'rsp'))
- key_grad: bfloat16 [32768, 1024], P(('ctx', 'rsp'))
- value_grad: bfloat16 [32768, 1024], P(('ctx', 'rsp'))
All inputs are finite; a program needn't handle non-finite values.
Results may differ from a plain program's by a relative error of at most 0.0077.
Values may be sent and summed in bfloat16 or wider, within the bound.
A program may use at most 64 MiB of HBM per device.

v0:
```python
import jax
import jax.numpy as jnp
from jax import lax
from jax.sharding import PartitionSpec as P

HEADS = 64
KV_HEADS = 8
HEAD_DIM = 128
RESPONSES = 16


def shifted(value, axis, steps):
    count = lax.axis_size(axis)
    pairs = [(source, (source + steps) % count) for source in range(count)]
    return lax.ppermute(value, axis, pairs)


def pick_entry(entries, position):
    matches = lax.broadcasted_iota(jnp.int32, entries.shape, 0) == position
    return jnp.sum(jnp.where(matches, entries, 0))


def tile_grads(queries, cotangent, lse_rows, delta_rows, keys, values, factor):
    row_count = queries.shape[0]
    key_count = keys.shape[0]
    per_kv = HEADS // KV_HEADS
    score_scale = HEAD_DIM ** (-0.5)
    head_queries = queries.reshape(row_count, KV_HEADS, per_kv, HEAD_DIM)
    cotangent_head_rows = cotangent.reshape(row_count, KV_HEADS, per_kv, HEAD_DIM)
    head_keys = keys.reshape(key_count, KV_HEADS, HEAD_DIM)
    head_values = values.reshape(key_count, KV_HEADS, HEAD_DIM)
    logit_scores = (
        jnp.einsum("xnoh,snh->xnos", head_queries, head_keys, preferred_element_type=jnp.float32)
        * score_scale
    )
    softmax_rows = jnp.exp(logit_scores - lse_rows.reshape(row_count, KV_HEADS, per_kv)[..., None])
    if factor is not None:
        softmax_rows = softmax_rows * factor
    lowered_rows = softmax_rows.astype(jnp.bfloat16)
    value_gradient = jnp.einsum(
        "mios,mioz->siz", lowered_rows, cotangent_head_rows, preferred_element_type=jnp.float32
    )
    probability_gradient = jnp.einsum(
        "xnoh,snh->xnos", cotangent_head_rows, head_values, preferred_element_type=jnp.float32
    )
    grad_score = softmax_rows * (
        probability_gradient - delta_rows.reshape(row_count, KV_HEADS, per_kv)[..., None]
    )
    lowered_score = grad_score.astype(jnp.bfloat16)
    key_gradient = (
        jnp.einsum(
            "mios,mioz->siz", lowered_score, head_queries, preferred_element_type=jnp.float32
        )
        * score_scale
    )
    query_gradient = (
        jnp.einsum("qxof,fxm->qxom", lowered_score, head_keys, preferred_element_type=jnp.float32)
        * score_scale
    )
    return (
        query_gradient.reshape(row_count, HEADS * HEAD_DIM),
        key_gradient.reshape(key_count, KV_HEADS * HEAD_DIM),
        value_gradient.reshape(key_count, KV_HEADS * HEAD_DIM),
    )


def body(
    prompt_keys,
    prompt_values,
    block_offsets,
    prompt_queries,
    prompt_cotangent,
    prompt_lse,
    prompt_delta,
    response_queries,
    response_cotangent,
    response_lse,
    response_delta,
    response_ids,
    advantages,
):
    own_quarter = jnp.stack((prompt_keys, prompt_values))
    own_block = lax.all_gather(own_quarter, "rsp", axis=1, tiled=True)
    arrived = shifted(own_block, "ctx", 1)
    keys_in = arrived[0]
    values_in = arrived[1]
    loop_size = lax.axis_size("ctx")
    my_index = lax.axis_index("ctx")
    source_index = (my_index + loop_size - 1) % loop_size
    own_offset = pick_entry(block_offsets, my_index)
    source_offset = pick_entry(block_offsets, source_index)
    visible = jnp.where(source_offset < own_offset, 1.0, 0.0).astype(jnp.float32)
    matches = (response_ids[:, None] == lax.broadcasted_iota(jnp.int32, (1, RESPONSES), 1)).astype(
        jnp.float32
    )
    weight = jnp.sum(matches * advantages[None, :], axis=1)
    weighted = (weight[:, None] * response_cotangent.astype(jnp.float32)).astype(jnp.bfloat16)
    weighted_delta = weight[:, None] * response_delta
    answer_dq, answer_dk, answer_dv = tile_grads(
        response_queries, weighted, response_lse, weighted_delta, keys_in, values_in, None
    )
    prompt_dq, prompt_dk, prompt_dv = tile_grads(
        prompt_queries, prompt_cotangent, prompt_lse, prompt_delta, keys_in, values_in, visible
    )
    partials = jnp.stack((answer_dk + prompt_dk, answer_dv + prompt_dv))
    summed = lax.psum_scatter(partials.astype(jnp.bfloat16), "rsp", scatter_dimension=1, tiled=True)
    returned = shifted(summed, "ctx", -1)
    return (
        answer_dq.astype(jnp.bfloat16),
        prompt_dq.astype(jnp.bfloat16),
        returned[0],
        returned[1],
    )


def solution(mesh):
    return jax.shard_map(
        body,
        mesh=mesh,
        in_specs=(
            P(("ctx", "rsp"), None),
            P(("ctx", "rsp"), None),
            P(),
            P(("ctx", "rsp"), None),
            P(("ctx", "rsp"), None),
            P(("ctx", "rsp"), None),
            P(("ctx", "rsp"), None),
            P(("ctx", "rsp"), None),
            P(("ctx", "rsp"), None),
            P(("ctx", "rsp"), None),
            P(("ctx", "rsp"), None),
            P(("ctx", "rsp")),
            P(),
        ),
        out_specs=(
            P(("ctx", "rsp"), None),
            P(("ctx", "rsp"), None),
            P(("ctx", "rsp"), None),
            P(("ctx", "rsp"), None),
        ),
        check_vma=False,
    )
```

profile of v0, /device:TPU:126, one launch (start us, length us, event | category | flops | bytes accessed | tf_op | source)
XLA Modules:
  0.0 119.7 jit_solution(2613636765691170685)
XLA Ops:
  7.2 0.0 all-gather.2.cloned.1.call-start
  7.2 1.2 copy.58
  8.4 1.1 copy.59
  9.6 0.8 pad_maximum_fusion.1
  10.4 0.0 all-gather.2.cloned.1.call-update
  10.4 0.0 reduce-scatter.2.cloned.1.call-start
  10.5 16.0 %all-gather.2.cloned.1.call-done = bf16[2,256,1024]{1,2,0:T(8,128)(2,1)} async-done(((bf16[2,128,1024]{1,2,0:T(8,128)(2,1)}), bf16[2,256,1024]{1,2,0:T(8,128)(2,1)}) %all-gather.2.cloned.1.call-update) | async-done | bytes 1048592 | tf_op jit(solution)/shard_map/all_gather | solution.py:83
  26.5 2.7 %collective-permute-start = (bf16[2,256,1024]{1,2,0:T(8,128)(2,1)}, bf16[2,256,1024]{1,2,0:T(8,128)(2,1)}, u32[]{:S(2)}, u32[]{:S(2)}) collective-permute-start(bf16[2,256,1024]{1,2,0:T(8,128)(2,1)} %all-gather.2.cloned.1.call-done), channel_id=1, source_target_pairs={{0,2},{2,4},{4,6},{6,8},{8,10},{10,12},{12,14},{14,16},{16,18},{18... | collective-permute-start | bytes 3145736 | tf_op jit(solution)/shard_map/ppermute | solution.py:15
  29.2 0.8 copy.62
  30.0 0.8 copy.65
  30.8 0.8 select_reduce_fusion
  31.6 1.5 %fusion.32 = bf16[8,8,64,128]{3,1,2,0:T(8,128)(2,1)S(1)} fusion(bf16[64,8192]{1,0:T(8,128)(2,1)} %param.21, f32[64]{0:T(128)S(1)} %select_reduce_fusion), kind=kLoop, calls=%fused_computation.32 | loop fusion | flops 1572864 | bytes 2097408
  33.1 1.2 %copy.107 = bf16[8,8,64,128]{3,2,1,0:T(8,128)(2,1)} copy(bf16[8,8,64,128]{3,1,2,0:T(8,128)(2,1)S(1)} %fusion.32) | data formatting | bytes 2097152
  34.4 1.3 %copy.106 = bf16[8,8,64,128]{3,2,1,0:T(8,128)(2,1)} copy(bf16[8,8,64,128]{3,1,2,0:T(8,128)(2,1)S(1)} %bitcast.141) | data formatting | bytes 2097152
  35.6 3.2 %copy.104 = bf16[128,8192]{0,1:T(8,128)(2,1)S(1)} copy(bf16[128,8192]{1,0:T(8,128)(2,1)} %param.16) | data formatting | bytes 4194304 | tf_op jit(solution)/shard_map/reshape | solution.py:28
  38.9 4.1 %copy.105 = bf16[128,8192]{0,1:T(8,128)(2,1)} copy(bf16[128,8192]{1,0:T(8,128)(2,1)} %param.17) | data formatting | bytes 4194304 | tf_op jit(solution)/shard_map/reshape | solution.py:29
  42.9 0.0 copy-done.8
  42.9 0.6 fusion.38
  44.9 7.4 %collective-permute-done = bf16[2,256,1024]{1,2,0:T(8,128)(2,1)} collective-permute-done((bf16[2,256,1024]{1,2,0:T(8,128)(2,1)}, bf16[2,256,1024]{1,2,0:T(8,128)(2,1)}, u32[]{:S(2)}, u32[]{:S(2)}) %collective-permute-start) | collective-permute-done | bytes 1048608 | tf_op jit(solution)/shard_map/ppermute | solution.py:15
  52.3 1.3 %fusion.40 = (bf16[1,256,1024]{1,2,0:T(8,128)(2,1)S(1)}, bf16[1,256,1024]{1,2,0:T(8,128)(2,1)S(1)}) fusion(bf16[2,256,1024]{1,2,0:T(8,128)(2,1)} %collective-permute-done), kind=kLoop, calls=%fused_computation.50 | loop fusion | bytes 2097152 | tf_op jit(solution)/shard_map/slice | solution.py:86
  53.6 0.0 copy-start.4
  53.6 0.0 copy-start.7
  53.6 1.3 %fusion.41 = f32[8,256,128,8]{2,1,3,0:T(8,128)S(1)} fusion(bf16[256,8,128,1]{0,2,3,1:T(8,128)(2,1)S(1)} %bitcast.125, bf16[128,8,8,128]{0,3,2,1:T(8,128)(2,1)S(1)} %bitcast.123), kind=kOutput, calls=%fused_computation.51 | convolution fusion | flops 536870912 | bytes 11010048 | tf_op jit(solution)/shard_map/xnoh,snh->xnos/dot_general | solution.py:33
  54.9 0.3 copy-done.4
  55.2 2.9 %fusion.20 = f32[256,8,128]{0,2,1:T(8,128)} fusion(bf16[128,8,8,128]{0,3,2,1:T(8,128)(2,1)S(1)} %bitcast.134, f32[8,256,128,8]{2,1,3,0:T(8,128)S(1)} %fusion.41, f32[]{:T(128)S(6)} %select_n.21, f32[128,8,8]{0,2,1:T(8,128)S(1)} %bitcast.148), kind=kOutput, calls=%fused_computation.24 | convolution fusion | flops 545259520 | bytes 11567108 | tf_op jit(solution)/shard_map/mios,mioz->siz/dot_general | solution.py:40
  58.1 2.7 %fusion.1 = bf16[128,8,8,256]{0,3,2,1:T(8,128)(2,1)S(1)} fusion(f32[8,256,128,8]{2,1,3,0:T(8,128)S(1)} %fusion.41, f32[128,8,8]{0,2,1:T(8,128)S(1)} %bitcast.147, f32[]{:T(128)S(6)} %select_n.21, f32[128,8,8]{0,2,1:T(8,128)S(1)} %bitcast.149, bf16[256,8,128,1]{0,2,3,1:T(8,128)(2,1)S(1)} %bitcast.136, bf16[128,8,8,128]{0,3,2,1:T(8,128)(2,1)S(1)} %bitcast.135), kind=kOutput, calls=%fused_computation.2 | convolution fusion | flops 549453824 | bytes 15269892 | tf_op jit(solution)/shard_map/xnoh,snh->xnos/dot_general | solution.py:43
  60.8 0.0 copy-start
  60.8 0.0 copy-start.3
  60.8 1.5 %convolution_bitcast_fusion = f32[8,256,128]{1,2,0:T(8,128)S(1)} fusion(bf16[128,8,8,256]{0,3,2,1:T(8,128)(2,1)S(1)} %fusion.1, bf16[128,8,8,128]{0,3,2,1:T(8,128)(2,1)S(1)} %bitcast.124), kind=kOutput, calls=%fused_computation.25 | convolution fusion | flops 536870912 | bytes 7340032 | tf_op jit(solution)/shard_map/mios,mioz->siz/dot_general | solution.py:51
  62.3 0.5 copy-done.3
  62.8 2.4 %fusion.13 = (bf16[64,8,8,256]{3,0,2,1:T(8,128)(2,1)}, f32[8,256,64,8]{1,2,3,0:T(8,128)S(1)}) fusion(f32[64,8,8]{0,2,1:T(8,128)S(1)} %bitcast.145, bf16[256,8,128,1]{0,2,3,1:T(8,128)(2,1)S(1)} %bitcast.126, bf16[64,8,8,128]{3,2,1,0:T(8,128)(2,1)S(1)} %bitcast.131), kind=kOutput, calls=%fused_computation.17 | convolution fusion | flops 271581184 | bytes 7880704 | tf_op jit(solution)/shard_map/xnoh,snh->xnos/dot_general | solution.py:33
  65.3 1.8 %fusion.8 = bf16[64,8,8,256]{3,0,2,1:T(8,128)(2,1)S(1)} fusion(f32[8,256,64,8]{1,2,3,0:T(8,128)S(1)} %get-tuple-element.23, bf16[256,8,128,1]{0,2,3,1:T(8,128)(2,1)S(1)} %bitcast.137, f32[64,8,8]{0,2,1:T(8,128)S(1)} %multiply_bitcast_fusion, f32[64,8,8]{0,2,1:T(8,128)S(1)} %bitcast.146, bf16[64,8,8,128]{3,2,1,0:T(8,128)(2,1)S(1)} %bitcast.130), kind=kOutput, calls=%fused_computation.10 | convolution fusion | flops 273678336 | bytes 7897088 | tf_op jit(solution)/shard_map/xnoh,snh->xnos/dot_general | solution.py:43
  67.1 1.5 %fusion.28 = bf16[8,256,128]{1,2,0:T(8,128)(2,1)S(1)} fusion(f32[8,256,128]{1,2,0:T(8,128)S(1)} %convolution_bitcast_fusion, bf16[64,8,8,256]{3,0,2,1:T(8,128)(2,1)S(1)} %fusion.8, bf16[64,8,8,128]{3,2,1,0:T(8,128)(2,1)S(1)} %bitcast.132), kind=kOutput, calls=%fused_computation.30 | convolution fusion | flops 269221888 | bytes 4718592 | tf_op jit(solution)/shard_map/mios,mioz->siz/dot_general | solution.py:51
  68.6 1.0 copy.79
  69.6 3.6 %fusion.29 = bf16[256,8,128]{0,2,1:T(8,128)(2,1)S(1)} fusion(f32[256,8,128]{0,2,1:T(8,128)} %fusion.20, bf16[64,8,8,128]{3,2,1,0:T(8,128)(2,1)} %bitcast.129, bf16[64,8,8,256]{3,0,2,1:T(8,128)(2,1)} %get-tuple-element.22), kind=kOutput, calls=%fused_computation.31 | convolution fusion | flops 268959744 | bytes 4718592 | tf_op jit(solution)/shard_map/mios,mioz->siz/dot_general | solution.py:40
  73.3 1.0 copy.80
  74.3 2.3 %pad_maximum_fusion = bf16[2,256,1024]{2,1,0:T(8,128)(2,1)} fusion(bf16[1,256,1024]{2,1,0:T(8,128)(2,1)} %copy.80, bf16[1,256,1024]{2,1,0:T(8,128)(2,1)} %copy.79), kind=kLoop, calls=%fused_computation.34 | loop fusion | flops 524288 | bytes 2097152 | tf_op jit(solution)/shard_map/stack | solution.py:105
  76.6 0.0 reduce-scatter.2.cloned.1.call-update
  76.6 15.7 %reduce-scatter.2.cloned.1.call-done = bf16[2,128,1024]{2,1,0:T(8,128)(2,1)} async-done(((bf16[2,256,1024]{2,1,0:T(8,128)(2,1)}), bf16[2,128,1024]{2,1,0:T(8,128)(2,1)}) %reduce-scatter.2.cloned.1.call-update) | async-done | bytes 524304 | tf_op jit(solution)/shard_map/reduce_scatter | solution.py:106
  92.3 0.9 collective-permute-start.1
  93.1 0.7 fusion.16
  93.8 0.7 copy.67
  94.5 1.7 %copy.126 = bf16[8,8,64,128]{3,1,2,0:T(8,128)(2,1)} copy(bf16[8,8,64,128]{3,2,1,0:T(8,128)(2,1)S(1)} %bitcast.138) | data formatting | bytes 2097152
  96.2 0.0 copy-done.1
  96.2 0.8 multiply_convert_fusion
  97.0 2.9 %copy.81 = bf16[128,8192]{1,0:T(8,128)(2,1)} copy(bf16[128,8192]{0,1:T(8,128)(2,1)S(1)} %bitcast.133) | data formatting | bytes 4194304
  99.9 12.2 %collective-permute-done.1 = bf16[2,128,1024]{2,1,0:T(8,128)(2,1)S(1)} collective-permute-done((bf16[2,128,1024]{2,1,0:T(8,128)(2,1)}, bf16[2,128,1024]{2,1,0:T(8,128)(2,1)S(1)}, u32[]{:S(2)}, u32[]{:S(2)}) %collective-permute-start.1) | collective-permute-done | bytes 524320 | tf_op jit(solution)/shard_map/ppermute | solution.py:15
  112.1 0.8 slice_bitcast_fusion
  (11 shorter events, 0.0 us)
Async XLA Ops:
  7.2 27.2 %copy-start.5 = (bf16[64,8192]{1,0:T(8,128)(2,1)S(1)}, bf16[64,8192]{1,0:T(8,128)(2,1)}, u32[]{:S(2)}) copy-start(bf16[64,8192]{1,0:T(8,128)(2,1)} %param.20) | copy-start | bytes 3145732
  7.2 19.3 %all-gather.2.cloned.1.call-start = ((), (), s32[]{:S(2)}) async-start(), calls=%async_computation.1 | async-start | bytes 1572864 | tf_op jit(solution)/shard_map/all_gather | solution.py:83
  10.4 81.8 %reduce-scatter.2.cloned.1.call-start = ((), (), s32[]{:S(2)}) async-start(), calls=%async_computation.2 | async-start | bytes 1572864 | tf_op jit(solution)/shard_map/reduce_scatter | solution.py:106
  26.5 25.8 %collective-permute-start = (bf16[2,256,1024]{1,2,0:T(8,128)(2,1)}, bf16[2,256,1024]{1,2,0:T(8,128)(2,1)}, u32[]{:S(2)}, u32[]{:S(2)}) collective-permute-start(bf16[2,256,1024]{1,2,0:T(8,128)(2,1)} %all-gather.2.cloned.1.call-done), channel_id=1, source_target_pairs={{0,2},{2,4},{4,6},{6,8},{8,10},{10,12},{12,14},{14,16},{16,18},{18... | collective-permute-start | bytes 3145736 | tf_op jit(solution)/shard_map/ppermute | solution.py:15
  35.6 7.3 %copy-start.8 = (s32[128]{0:T(128)S(1)}, s32[128]{0:T(128)}, u32[]{:S(2)}) copy-start(s32[128]{0:T(128)} %param.15) | copy-start | bytes 1540
  53.6 1.6 %copy-start.4 = (bf16[128,8192]{0,1:T(8,128)(2,1)S(1)}, bf16[128,8192]{0,1:T(8,128)(2,1)}, u32[]{:S(2)}) copy-start(bf16[128,8192]{0,1:T(8,128)(2,1)} %copy.105) | copy-start | bytes 6291460
  53.6 1.6 %copy-start.7 = (f32[128,64]{0,1:T(8,128)S(1)}, f32[128,64]{0,1:T(8,128)}, u32[]{:S(2)}) copy-start(f32[128,64]{0,1:T(8,128)} %param.18) | copy-start | bytes 98308
  55.2 3.0 %copy-start.6 = (f32[128,64]{0,1:T(8,128)S(1)}, f32[128,64]{0,1:T(8,128)}, u32[]{:S(2)}) copy-start(f32[128,64]{0,1:T(8,128)} %param.19) | copy-start | bytes 98308
  60.8 4.5 %copy-start = (bf16[128,8,8,256]{0,3,2,1:T(8,128)(2,1)}, bf16[128,8,8,256]{0,3,2,1:T(8,128)(2,1)S(1)}, u32[]{:S(2)}) copy-start(bf16[128,8,8,256]{0,3,2,1:T(8,128)(2,1)S(1)} %fusion.1) | copy-start | bytes 12582916
  60.8 2.0 %copy-start.3 = (bf16[8,8,64,128]{3,2,1,0:T(8,128)(2,1)S(1)}, bf16[8,8,64,128]{3,2,1,0:T(8,128)(2,1)}, u32[]{:S(2)}) copy-start(bf16[8,8,64,128]{3,2,1,0:T(8,128)(2,1)} %copy.106) | copy-start | bytes 3145732
  62.3 3.0 %copy-start.2 = (bf16[8,8,64,128]{3,2,1,0:T(8,128)(2,1)S(1)}, bf16[8,8,64,128]{3,2,1,0:T(8,128)(2,1)}, u32[]{:S(2)}) copy-start(bf16[8,8,64,128]{3,2,1,0:T(8,128)(2,1)} %copy.107) | copy-start | bytes 3145732
  92.3 4.0 %copy-start.1 = (bf16[128,8,8,256]{0,3,2,1:T(8,128)(2,1)S(1)}, bf16[128,8,8,256]{0,3,2,1:T(8,128)(2,1)}, u32[]{:S(2)}) copy-start(bf16[128,8,8,256]{0,3,2,1:T(8,128)(2,1)} %copy-done) | copy-start | bytes 12582916
  92.3 19.8 %collective-permute-start.1 = (bf16[2,128,1024]{2,1,0:T(8,128)(2,1)}, bf16[2,128,1024]{2,1,0:T(8,128)(2,1)S(1)}, u32[]{:S(2)}, u32[]{:S(2)}) collective-permute-start(bf16[2,128,1024]{2,1,0:T(8,128)(2,1)} %reduce-scatter.2.cloned.1.call-done), channel_id=1, source_target_pairs={{0,254},{2,0},{4,2},{6,4},{8,6},{10,8},{12,10},{14,12},{16,14},{18... | collective-permute-start | bytes 1572872 | tf_op jit(solution)/shard_map/ppermute | solution.py:15
Sparse Core Ops, SparseCore 0:
  10.5 15.8 all-gather.1
  76.7 15.5 reduce-scatter.1
where the time goes:
time: 122 us; the launch traced here: 120 us
  waiting for transfers between devices  51.3 us (42%)
  local copies, waits for them, and re-layouts  24 us (20%)
  matrix products  19.2 us (16%)
  between operations  15.5 us (13%)
  other arithmetic  6.03 us (5%)
  starting transfers between devices  3.61 us (3%)
    ppermute x2, waiting for transfers between devices, shifted(): return lax.ppermute(value, axis, pairs)  19.6 us
    all_gather x1, waiting for transfers between devices, body(): own_block = lax.all_gather(own_quarter, 'rsp', axis=1, tiled=True)  16 us
    reduce_scatter x1, waiting for transfers between devices, body(): lax.psum_scatter(partials.astype(jnp.bfloat16), 'rsp', scatter_dimension=...  15.7 us
    unnamed x26, local copies, waits for them, and re-layouts  11.9 us
    dot_general x2, matrix products, tile_grads(): jnp.einsum('mios,mioz->siz', lowered_rows, cotangent_head_rows, preferred...  6.58 us
    dot_general x2, matrix products, tile_grads(): jnp.einsum('xnoh,snh->xnos', cotangent_head_rows, head_values, preferred_...  4.44 us
    reshape x1, local copies, waits for them, and re-layouts, tile_grads(): cotangent.reshape(row_count, KV_HEADS, per_kv, HEAD_DIM)  4.07 us
    dot_general x2, matrix products, tile_grads(): jnp.einsum('xnoh,snh->xnos', head_queries, head_keys, preferred_element_t...  3.73 us
  transfers between devices with their start and end apart: 4, of which 4 were waited for; matrix products, arithmetic and copies ran while one was open for 18% of the time, Pallas kernels for 0%

commit v1 on v0

v1 whole, which is shorter than its diff:
```python
import jax
import jax.numpy as jnp
from jax import lax
from jax.experimental import pallas as pl
from jax.experimental.pallas import tpu as pltpu
from jax.sharding import PartitionSpec as P

HEADS = 64
KV = 8
PER = HEADS // KV
DIM = 128
RESPONSES = 16
PROWS = 128
RROWS = 64
KEYS = 256
TILES = 6
SCALE = float(DIM**-0.5)
LOG2E = 1.4426950408889634
SCALE2 = SCALE * LOG2E
HIDDEN = 1e30
F32 = jnp.float32
BF16 = jnp.bfloat16
MESH = pl.DeviceIdType.MESH


def dot(a, b, ca, cb):
    return lax.dot_general(a, b, (((ca,), (cb,)), ((), ())), preferred_element_type=F32)


def kernel(
    pk, pv, offsets, pq, pc, plse, pdel, rq, rc, rlse, rdel, ids, adv,
    rgrad, pgrad, kvgrad,
    kvin, q_p, c_p, q_r, c_r, w_r,
    lp, ep, lr, er, lse_p, del_p, lse_r, del_r, ids_v, offsets_s, adv_s, square,
    probs, score_a, score_b, part, got, back,
    load_sem, small_sem, kv_send, kv_recv, fw_send, fw_recv,
    ex_send, ex_recv, back_send, back_recv,
):
    count = lax.axis_size("ctx")
    me = lax.axis_index("ctx")
    core = lax.axis_index("rsp")
    right = lax.rem(me + 1, count)
    left = lax.rem(me + count - 1, count)
    other = 1 - core
    mine = pl.ds(pl.multiple_of(core * PROWS, PROWS), PROWS)
    theirs = pl.ds(pl.multiple_of(other * PROWS, PROWS), PROWS)

    barrier = pltpu.get_barrier_semaphore()
    for device in ((left, core), (me, other)):
        pl.semaphore_signal(barrier, inc=1, device_id=device, device_id_type=MESH)

    small = [
        pltpu.make_async_copy(source, target, small_sem.at[i])
        for i, (source, target) in enumerate(
            (
                (ids, ids_v), (plse, lse_p), (pdel, del_p), (rlse, lse_r),
                (rdel, del_r), (offsets, offsets_s), (adv, adv_s),
            )
        )
    ]
    loads = [
        pltpu.make_async_copy(source, target, load_sem.at[i])
        for i, (source, target) in enumerate(((rc, c_r), (pq, q_p), (pc, c_p), (rq, q_r)))
    ]
    for copy in small:
        copy.start()

    def send_kv(n):
        columns = pl.ds(pl.multiple_of(n * DIM, DIM), DIM)
        return [
            pltpu.make_async_remote_copy(
                src_ref=source.at[:, columns],
                dst_ref=kvin.at[n, i, mine, :],
                send_sem=kv_send.at[i, n],
                recv_sem=kv_recv.at[i, n],
                device_id=(right, core),
                device_id_type=MESH,
            )
            for i, source in enumerate((pk, pv))
        ]

    def kv_arrived(n):
        for copy in send_kv(n):
            copy.wait_recv()

    def forward(n):
        return pltpu.make_async_remote_copy(
            src_ref=kvin.at[n, :, mine, :],
            dst_ref=kvin.at[n, :, mine, :],
            send_sem=fw_send.at[n],
            recv_sem=fw_recv.at[n],
            device_id=(me, other),
            device_id_type=MESH,
        )

    def exchange(n):
        return pltpu.make_async_remote_copy(
            src_ref=part.at[n, :, theirs, :],
            dst_ref=got.at[n],
            send_sem=ex_send.at[n],
            recv_sem=ex_recv.at[n],
            device_id=(me, other),
            device_id_type=MESH,
        )

    def give_back(n):
        return pltpu.make_async_remote_copy(
            src_ref=back.at[n],
            dst_ref=kvgrad.at[:, :, pl.ds(pl.multiple_of(n * DIM, DIM), DIM)],
            send_sem=back_send.at[n],
            recv_sem=back_recv.at[n],
            device_id=(left, core),
            device_id_type=MESH,
        )

    pl.semaphore_wait(barrier, 2)
    for n in range(KV):
        for copy in send_kv(n):
            copy.start()
    for copy in loads:
        copy.start()

    for copy in small:
        copy.wait()
    visible = offsets_s[left] < offsets_s[me]
    weight_row = jnp.zeros((1, RROWS), F32)
    for j in range(RESPONSES):
        weight_row = weight_row + jnp.where(ids_v[...] == j, adv_s[j], 0.0)
    square[...] = jnp.zeros_like(square)
    square[:, 0:RROWS] = jnp.broadcast_to(weight_row, (PROWS, RROWS))
    weight = square[...].T[0:RROWS, :]

    def turned(top, bottom):
        square[0:RROWS, 0:HEADS] = top
        square[RROWS:PROWS, 0:HEADS] = bottom
        return square[...].T

    def turned_response(values):
        return turned(values, jnp.concatenate((values[:, 4:], values[:, :4]), axis=1))

    lse_t = jnp.where(visible, lse_p[...] * LOG2E, HIDDEN)
    del_t = del_p[...]
    rlse_t = turned_response(lse_r[...]) * LOG2E
    rdel_t = turned_response(del_r[...] * weight[:, 0:HEADS])
    for n in range(KV):
        lp[n] = lse_t[n * PER : (n + 1) * PER]
        ep[n] = del_t[n * PER : (n + 1) * PER]
        lr[n] = rlse_t[n * PER : (n + 1) * PER]
        er[n] = rdel_t[n * PER : (n + 1) * PER]

    for copy in loads:
        copy.wait()

    def weigh(i, carry):
        columns = pl.ds(pl.multiple_of(i * DIM, DIM), DIM)
        w_r[:, columns] = (weight * c_r[:, columns].astype(F32)).astype(BF16)
        return carry

    lax.fori_loop(0, HEADS, weigh, 0)

    def spans(n, t):
        if t < 4:
            heads = (2 * t, 2 * t + 1)
        else:
            u = (t - 4) * 2
            heads = (u, u + 4, u + 1, u + 5)
        return [pl.ds(pl.multiple_of(n * PER * DIM + h * DIM, DIM), DIM) for h in heads]

    def rows_of(n, t, prompt, response):
        source = prompt if t < 4 else response
        return jnp.concatenate([source[:, columns] for columns in spans(n, t)], axis=0)

    def stats_of(n, t, prompt, response):
        source, first = (prompt, 2 * t) if t < 4 else (response, (t - 4) * 2)
        return jnp.concatenate((source[n, first : first + 1, :], source[n, first + 1 : first + 2, :]), axis=1)

    def scores(n, t, score):
        span = pl.ds(t * KEYS, KEYS)
        st = dot(kvin[n, 0], rows_of(n, t, q_p, q_r), 1, 1)
        gt = dot(kvin[n, 1], rows_of(n, t, c_p, w_r), 1, 1)
        p = jnp.exp2(st * SCALE2 - stats_of(n, t, lp, lr))
        probs[:, span] = p.astype(BF16)
        score[:, span] = (p * (gt - stats_of(n, t, ep, er))).astype(BF16)

    def query_grads(n, t, score):
        grad = dot(kvin[n, 0].T, score[:, pl.ds(t * KEYS, KEYS)], 1, 0)
        grad = (grad.T * SCALE).astype(BF16)
        target, rows = (pgrad, PROWS) if t < 4 else (rgrad, RROWS)
        for i, columns in enumerate(spans(n, t)):
            target[:, columns] = grad[i * rows : (i + 1) * rows]

    def key_grads(n, score):
        queries = jnp.concatenate([rows_of(n, t, q_p, q_r) for t in range(TILES)], axis=0)
        cotangent = jnp.concatenate([rows_of(n, t, c_p, w_r) for t in range(TILES)], axis=0)
        part[n, 1] = dot(probs[...], cotangent, 1, 0).astype(BF16)
        part[n, 0] = (dot(score[...], queries, 1, 0) * SCALE).astype(BF16)

    def send_sum(n):
        exchange(n).wait_recv()
        back[n] = (part[n, :, mine, :].astype(F32) + got[n].astype(F32)).astype(BF16)
        give_back(n).start()

    def step(n, score, before, first=False, last=False):
        if not (first or last):
            kv_arrived(n + 1)
            forward(n + 1).start()
        forward(n).wait_recv()
        for t in range(TILES):
            if first and t == TILES // 2:
                kv_arrived(n + 1)
                forward(n + 1).start()
            scores(n, t, score)
            if not first:
                query_grads(n - 1, t, before)
        key_grads(n, score)
        exchange(n).start()
        if not first:
            send_sum(n - 1)

    kv_arrived(0)
    forward(0).start()
    step(0, score_a, score_b, first=True)

    def pair(m, carry):
        step(2 * m + 1, score_b, score_a)
        step(2 * m + 2, score_a, score_b)
        return carry

    lax.fori_loop(0, (KV - 2) // 2, pair, 0)
    step(KV - 1, score_b, score_a, last=True)
    for t in range(TILES):
        query_grads(KV - 1, t, score_b)
    send_sum(KV - 1)

    def finish(n, carry):
        for copy in send_kv(n):
            copy.wait_send()
        forward(n).wait_send()
        exchange(n).wait_send()
        give_back(n).wait()
        return carry

    lax.fori_loop(0, KV, finish, 0)


def write_out(rgrad, pgrad, kvgrad, rgrad_out, pgrad_out, kgrad_out, vgrad_out, sems):
    copies = [
        pltpu.make_async_copy(source, target, sems.at[i])
        for i, (source, target) in enumerate(
            (
                (pgrad, pgrad_out), (rgrad, rgrad_out),
                (kvgrad.at[0], kgrad_out), (kvgrad.at[1], vgrad_out),
            )
        )
    ]
    for copy in copies:
        copy.start()
    for copy in copies:
        copy.wait()


def body(pk, pv, offsets, pq, pc, plse, pdel, rq, rc, rlse, rdel, ids, adv):
    main = pl.BlockSpec(memory_space=pltpu.HBM)
    vector = pl.BlockSpec(memory_space=pltpu.VMEM)
    wide = HEADS * DIM
    operands = (pk, pv, offsets, pq, pc, plse.T, pdel.T, rq, rc, rlse, rdel, ids.reshape(1, RROWS), adv)
    operands = [pltpu.with_memory_space_constraint(x, pltpu.HBM) for x in operands]
    rgrad, pgrad, kvgrad = pl.pallas_call(
        kernel,
        out_shape=(
            pltpu.VMEM((RROWS, wide), BF16),
            pltpu.VMEM((PROWS, wide), BF16),
            pltpu.VMEM((2, PROWS, KV * DIM), BF16),
        ),
        in_specs=[main] * 13,
        out_specs=(vector, vector, vector),
        scratch_shapes=[
            pltpu.VMEM((KV, 2, KEYS, DIM), BF16),
            pltpu.VMEM((PROWS, wide), BF16),
            pltpu.VMEM((PROWS, wide), BF16),
            pltpu.VMEM((RROWS, wide), BF16),
            pltpu.VMEM((RROWS, wide), BF16),
            pltpu.VMEM((RROWS, wide), BF16),
            pltpu.VMEM((KV, PER, PROWS), F32),
            pltpu.VMEM((KV, PER, PROWS), F32),
            pltpu.VMEM((KV, PER, PROWS), F32),
            pltpu.VMEM((KV, PER, PROWS), F32),
            pltpu.VMEM((HEADS, PROWS), F32),
            pltpu.VMEM((HEADS, PROWS), F32),
            pltpu.VMEM((RROWS, HEADS), F32),
            pltpu.VMEM((RROWS, HEADS), F32),
            pltpu.VMEM((1, RROWS), jnp.int32),
            pltpu.SMEM(offsets.shape, jnp.int32),
            pltpu.SMEM((RESPONSES,), F32),
            pltpu.VMEM((PROWS, PROWS), F32),
            pltpu.VMEM((KEYS, TILES * KEYS), BF16),
            pltpu.VMEM((KEYS, TILES * KEYS), BF16),
            pltpu.VMEM((KEYS, TILES * KEYS), BF16),
            pltpu.VMEM((KV, 2, KEYS, DIM), BF16),
            pltpu.VMEM((KV, 2, PROWS, DIM), BF16),
            pltpu.VMEM((KV, 2, PROWS, DIM), BF16),
            pltpu.SemaphoreType.DMA((4,)),
            pltpu.SemaphoreType.DMA((7,)),
            pltpu.SemaphoreType.DMA((2, KV)),
            pltpu.SemaphoreType.DMA((2, KV)),
            pltpu.SemaphoreType.DMA((KV,)),
            pltpu.SemaphoreType.DMA((KV,)),
            pltpu.SemaphoreType.DMA((KV,)),
            pltpu.SemaphoreType.DMA((KV,)),
            pltpu.SemaphoreType.DMA((KV,)),
            pltpu.SemaphoreType.DMA((KV,)),
        ],
        compiler_params=pltpu.CompilerParams(
            collective_id=0, has_side_effects=True, vmem_limit_bytes=28 * 2**20
        ),
        name="prefix_backward",
    )(*operands)
    grads = [pltpu.with_memory_space_constraint(x, pltpu.VMEM) for x in (rgrad, pgrad, kvgrad)]
    return pl.pallas_call(
        write_out,
        out_shape=(
            jax.ShapeDtypeStruct((RROWS, wide), BF16),
            jax.ShapeDtypeStruct((PROWS, wide), BF16),
            jax.ShapeDtypeStruct((PROWS, KV * DIM), BF16),
            jax.ShapeDtypeStruct((PROWS, KV * DIM), BF16),
        ),
        in_specs=[vector] * 3,
        out_specs=(main, main, main, main),
        scratch_shapes=[pltpu.SemaphoreType.DMA((4,))],
        compiler_params=pltpu.CompilerParams(vmem_limit_bytes=4 * 2**20),
        name="write_out",
    )(*grads)


def solution(mesh):
    rows = P(("ctx", "rsp"), None)
    return jax.shard_map(
        body,
        mesh=mesh,
        in_specs=(rows, rows, P(), rows, rows, rows, rows, rows, rows, rows, rows, P(("ctx", "rsp")), P()),
        out_specs=(rows, rows, rows, rows),
        check_vma=False,
    )
```

time: 122 us -> 33.5 us (0.27)
  the two profiles are of different devices: /device:TPU:126 before, /device:TPU:1 now
where the time goes in v1:
time: 33.5 us; the launch traced here: 33.4 us
  Pallas kernels  32.7 us (98%)
  between operations  0.64 us (2%)
    pallas_call x1, Pallas kernels, body(): pl.pallas_call(kernel, out_shape=(pltpu.VMEM((RROWS, wide), BF16), pltpu....  30.9 us
    pallas_call x1, Pallas kernels, body(): pl.pallas_call(write_out, out_shape=(jax.ShapeDtypeStruct((RROWS, wide),...  1.86 us

profile of v1, /device:TPU:1, one launch (start us, length us, event | category | flops | bytes accessed | tf_op | source)
XLA Modules:
  0.0 33.4 jit_solution(3911803545874981935)
XLA Ops:
  0.6 30.9 %prefix_backward.1 = (bf16[64,8192]{1,0:T(8,128)(2,1)S(1)}, bf16[128,8192]{1,0:T(8,128)(2,1)S(1)}, bf16[2,128,1024]{2,1,0:T(8,128)(2,1)S(1)}) custom-call(bf16[128,1024]{1,0:T(8,128)(2,1)} %pk.1, bf16[128,1024]{1,0:T(8,128)(2,1)} %pv.1, s32[128]{0:T(128)} %offsets.1, bf16[128,8192]{1,0:T(8,128)(2,1)} %pq.1, bf16[128,8192]{1,0:T(8,128)(2,1)} %pc.1, ...), custom_call_target="tpu_custom_call" | custom-call | tf_op jit(solution)/shard_map/prefix_backward/pallas_call | solution.py:268
  31.5 1.9 %write_out.1 = (bf16[64,8192]{1,0:T(8,128)(2,1)}, bf16[128,8192]{1,0:T(8,128)(2,1)}, bf16[128,1024]{1,0:T(8,128)(2,1)}, bf16[128,1024]{1,0:T(8,128)(2,1)}) custom-call(bf16[64,8192]{1,0:T(8,128)(2,1)S(1)} %get-tuple-element.7.rgrad, bf16[128,8192]{1,0:T(8,128)(2,1)S(1)} %get-tuple-element.8.pgrad, bf16[2,128,1024]{2,1,0:T(8,128)(2,1)S(1)} %get-tuple-element.9.kvgrad), custom_call_target="tpu_custom_call" | custom-call | tf_op jit(solution)/shard_map/write_out/pallas_call | solution.py:319

commit v2 on v1

--- a/solution.py
+++ b/solution.py
@@ -32,9 +32,9 @@
     rgrad, pgrad, kvgrad,
     kvin, q_p, c_p, q_r, c_r, w_r,
     lp, ep, lr, er, lse_p, del_p, lse_r, del_r, ids_v, offsets_s, adv_s, square,
-    probs, score_a, score_b, part, got, back,
+    probs, score_a, score_b, part, got, back, final, final_got,
     load_sem, small_sem, kv_send, kv_recv, fw_send, fw_recv,
-    ex_send, ex_recv, back_send, back_recv,
+    ex_send, ex_recv, back_send, back_recv, last_send,
 ):
     count = lax.axis_size("ctx")
     me = lax.axis_index("ctx")
@@ -103,6 +103,26 @@
             device_id_type=MESH,
         )
 
+    def hand_over():
+        return pltpu.make_async_remote_copy(
+            src_ref=part.at[KV - 1],
+            dst_ref=final_got,
+            send_sem=ex_send.at[KV - 1],
+            recv_sem=ex_recv.at[KV - 1],
+            device_id=(me, 0),
+            device_id_type=MESH,
+        )
+
+    def give_last(target):
+        return pltpu.make_async_remote_copy(
+            src_ref=final.at[:, pl.ds(target * PROWS, PROWS), :],
+            dst_ref=kvgrad.at[:, :, pl.ds((KV - 1) * DIM, DIM)],
+            send_sem=last_send.at[target],
+            recv_sem=back_recv.at[KV - 1],
+            device_id=(left, target),
+            device_id_type=MESH,
+        )
+
     def give_back(n):
         return pltpu.make_async_remote_copy(
             src_ref=back.at[n],
@@ -184,15 +204,17 @@
 
     def query_grads(n, t, score):
         grad = dot(kvin[n, 0].T, score[:, pl.ds(t * KEYS, KEYS)], 1, 0)
-        grad = (grad.T * SCALE).astype(BF16)
+        grad = (grad * SCALE).astype(BF16).T
         target, rows = (pgrad, PROWS) if t < 4 else (rgrad, RROWS)
         for i, columns in enumerate(spans(n, t)):
             target[:, columns] = grad[i * rows : (i + 1) * rows]
 
+    def value_grads(n):
+        cotangent = jnp.concatenate([rows_of(n, t, c_p, w_r) for t in range(TILES)], axis=0)
+        part[n, 1] = dot(probs[...], cotangent, 1, 0).astype(BF16)
+
     def key_grads(n, score):
         queries = jnp.concatenate([rows_of(n, t, q_p, q_r) for t in range(TILES)], axis=0)
-        cotangent = jnp.concatenate([rows_of(n, t, c_p, w_r) for t in range(TILES)], axis=0)
-        part[n, 1] = dot(probs[...], cotangent, 1, 0).astype(BF16)
         part[n, 0] = (dot(score[...], queries, 1, 0) * SCALE).astype(BF16)
 
     def send_sum(n):
@@ -212,8 +234,10 @@
             scores(n, t, score)
             if not first:
                 query_grads(n - 1, t, before)
+        value_grads(n)
         key_grads(n, score)
-        exchange(n).start()
+        if not last:
+            exchange(n).start()
         if not first:
             send_sum(n - 1)
 
@@ -228,19 +252,45 @@
 
     lax.fori_loop(0, (KV - 2) // 2, pair, 0)
     step(KV - 1, score_b, score_a, last=True)
+
+    @pl.when(core == 1)
+    def _():
+        hand_over().start()
+
     for t in range(TILES):
         query_grads(KV - 1, t, score_b)
-    send_sum(KV - 1)
+
+    @pl.when(core == 0)
+    def _():
+        hand_over().wait_recv()
+        final[...] = (part[KV - 1].astype(F32) + final_got[...].astype(F32)).astype(BF16)
+        for target in range(2):
+            give_last(target).start()
 
     def finish(n, carry):
         for copy in send_kv(n):
             copy.wait_send()
         forward(n).wait_send()
-        exchange(n).wait_send()
-        give_back(n).wait()
+
+        @pl.when(n < KV - 1)
+        def _():
+            exchange(n).wait_send()
+            give_back(n).wait()
+
         return carry
 
     lax.fori_loop(0, KV, finish, 0)
+
+    @pl.when(core == 1)
+    def _():
+        hand_over().wait_send()
+
+    @pl.when(core == 0)
+    def _():
+        for target in range(2):
+            give_last(target).wait_send()
+
+    give_last(0).wait_recv()
 
 
 def write_out(rgrad, pgrad, kvgrad, rgrad_out, pgrad_out, kgrad_out, vgrad_out, sems):
@@ -299,6 +349,8 @@
             pltpu.VMEM((KV, 2, KEYS, DIM), BF16),
             pltpu.VMEM((KV, 2, PROWS, DIM), BF16),
             pltpu.VMEM((KV, 2, PROWS, DIM), BF16),
+            pltpu.VMEM((2, KEYS, DIM), BF16),
+            pltpu.VMEM((2, KEYS, DIM), BF16),
             pltpu.SemaphoreType.DMA((4,)),
             pltpu.SemaphoreType.DMA((7,)),
             pltpu.SemaphoreType.DMA((2, KV)),
@@ -309,6 +361,7 @@
             pltpu.SemaphoreType.DMA((KV,)),
             pltpu.SemaphoreType.DMA((KV,)),
             pltpu.SemaphoreType.DMA((KV,)),
+            pltpu.SemaphoreType.DMA((2,)),
         ],
         compiler_params=pltpu.CompilerParams(
             collective_id=0, has_side_effects=True, vmem_limit_bytes=28 * 2**20

time: 33.5 us -> 32.9 us (0.982)
  the two profiles are of different devices: /device:TPU:1 before, /device:TPU:127 now
where the time goes in v2:
time: 32.9 us; the launch traced here: 32.8 us
  Pallas kernels  32.1 us (98%)
  between operations  0.64 us (2%)
    pallas_call x1, Pallas kernels, body(): pl.pallas_call(kernel, out_shape=(pltpu.VMEM((RROWS, wide), BF16), pltpu....  30.3 us
    pallas_call x1, Pallas kernels, body(): pl.pallas_call(write_out, out_shape=(jax.ShapeDtypeStruct((RROWS, wide),...  1.86 us

profile of v2, /device:TPU:127, one launch (start us, length us, event | category | flops | bytes accessed | tf_op | source)
XLA Modules:
  0.0 32.8 jit_solution(14271271915499822159)
XLA Ops:
  0.6 30.3 %prefix_backward.1 = (bf16[64,8192]{1,0:T(8,128)(2,1)S(1)}, bf16[128,8192]{1,0:T(8,128)(2,1)S(1)}, bf16[2,128,1024]{2,1,0:T(8,128)(2,1)S(1)}) custom-call(bf16[128,1024]{1,0:T(8,128)(2,1)} %pk.1, bf16[128,1024]{1,0:T(8,128)(2,1)} %pv.1, s32[128]{0:T(128)} %offsets.1, bf16[128,8192]{1,0:T(8,128)(2,1)} %pq.1, bf16[128,8192]{1,0:T(8,128)(2,1)} %pc.1, ...), custom_call_target="tpu_custom_call" | custom-call | tf_op jit(solution)/shard_map/prefix_backward/pallas_call | solution.py:318
  30.9 1.9 %write_out.1 = (bf16[64,8192]{1,0:T(8,128)(2,1)}, bf16[128,8192]{1,0:T(8,128)(2,1)}, bf16[128,1024]{1,0:T(8,128)(2,1)}, bf16[128,1024]{1,0:T(8,128)(2,1)}) custom-call(bf16[64,8192]{1,0:T(8,128)(2,1)S(1)} %get-tuple-element.7.rgrad, bf16[128,8192]{1,0:T(8,128)(2,1)S(1)} %get-tuple-element.8.pgrad, bf16[2,128,1024]{2,1,0:T(8,128)(2,1)S(1)} %get-tuple-element.9.kvgrad), custom_call_target="tpu_custom_call" | custom-call | tf_op jit(solution)/shard_map/write_out/pallas_call | solution.py:372

commit v3 on v1

--- a/solution.py
+++ b/solution.py
@@ -8,6 +8,8 @@
 HEADS = 64
 KV = 8
 PER = HEADS // KV
+LATE = KV - 2
+LAST = KV - 1
 DIM = 128
 RESPONSES = 16
 PROWS = 128
@@ -30,11 +32,11 @@
 def kernel(
     pk, pv, offsets, pq, pc, plse, pdel, rq, rc, rlse, rdel, ids, adv,
     rgrad, pgrad, kvgrad,
-    kvin, q_p, c_p, q_r, c_r, w_r,
+    kvsrc, kvin, q_p, c_p, q_r, c_r, w_r,
     lp, ep, lr, er, lse_p, del_p, lse_r, del_r, ids_v, offsets_s, adv_s, square,
-    probs, score_a, score_b, part, got, back,
-    load_sem, small_sem, kv_send, kv_recv, fw_send, fw_recv,
-    ex_send, ex_recv, back_send, back_recv,
+    probs, score_a, score_b, part, got, back, final, final_got,
+    first_send, stage_sem, load_sem, small_sem, kv_send, kv_recv, fw_send, fw_recv,
+    ex_send, ex_recv, back_send, back_recv, last_send,
 ):
     count = lax.axis_size("ctx")
     me = lax.axis_index("ctx")
@@ -42,6 +44,10 @@
     right = lax.rem(me + 1, count)
     left = lax.rem(me + count - 1, count)
     other = 1 - core
+    lead = (count - 1 - me) // (count - 1)
+    tail = me // (count - 1)
+    chosen = 1 - lead
+    late_from = KV - 1 - lead
     mine = pl.ds(pl.multiple_of(core * PROWS, PROWS), PROWS)
     theirs = pl.ds(pl.multiple_of(other * PROWS, PROWS), PROWS)
 
@@ -62,26 +68,31 @@
         pltpu.make_async_copy(source, target, load_sem.at[i])
         for i, (source, target) in enumerate(((rc, c_r), (pq, q_p), (pc, c_p), (rq, q_r)))
     ]
-    for copy in small:
+    stage = [pltpu.make_async_copy(source, kvsrc.at[i], stage_sem.at[i]) for i, source in enumerate((pk, pv))]
+    for copy in stage + small:
         copy.start()
 
     def send_kv(n):
-        columns = pl.ds(pl.multiple_of(n * DIM, DIM), DIM)
-        return [
-            pltpu.make_async_remote_copy(
-                src_ref=source.at[:, columns],
-                dst_ref=kvin.at[n, i, mine, :],
-                send_sem=kv_send.at[i, n],
-                recv_sem=kv_recv.at[i, n],
-                device_id=(right, core),
-                device_id_type=MESH,
-            )
-            for i, source in enumerate((pk, pv))
-        ]
-
-    def kv_arrived(n):
-        for copy in send_kv(n):
-            copy.wait_recv()
+        return pltpu.make_async_remote_copy(
+            src_ref=kvsrc.at[:, :, pl.ds(pl.multiple_of(n * DIM, DIM), DIM)],
+            dst_ref=kvin.at[n, :, mine, :],
+            send_sem=kv_send.at[n],
+            recv_sem=kv_recv.at[n],
+            device_id=(right, core),
+            device_id_type=MESH,
+        )
+
+    first_kv = [
+        pltpu.make_async_remote_copy(
+            src_ref=source.at[:, pl.ds(0, DIM)],
+            dst_ref=kvin.at[0, i, mine, :],
+            send_sem=first_send.at[i],
+            recv_sem=kv_recv.at[0],
+            device_id=(right, core),
+            device_id_type=MESH,
+        )
+        for i, source in enumerate((pk, pv))
+    ]
 
     def forward(n):
         return pltpu.make_async_remote_copy(
@@ -103,6 +114,27 @@
             device_id_type=MESH,
         )
 
+    def hand_over(n):
+        return pltpu.make_async_remote_copy(
+            src_ref=part.at[n],
+            dst_ref=final_got.at[n - LATE],
+            send_sem=ex_send.at[n],
+            recv_sem=ex_recv.at[n],
+            device_id=(me, chosen),
+            device_id_type=MESH,
+        )
+
+    def give_last(n, i):
+        target = chosen if i == 0 else 1 - chosen
+        return pltpu.make_async_remote_copy(
+            src_ref=final.at[n - LATE, :, pl.ds(pl.multiple_of(target * PROWS, PROWS), PROWS), :],
+            dst_ref=kvgrad.at[:, :, pl.ds(pl.multiple_of(n * DIM, DIM), DIM)],
+            send_sem=last_send.at[n - LATE, i],
+            recv_sem=back_recv.at[n],
+            device_id=(left, target),
+            device_id_type=MESH,
+        )
+
     def give_back(n):
         return pltpu.make_async_remote_copy(
             src_ref=back.at[n],
@@ -114,9 +146,21 @@
         )
 
     pl.semaphore_wait(barrier, 2)
-    for n in range(KV):
-        for copy in send_kv(n):
+
+    @pl.when(tail == 1)
+    def _():
+        for copy in first_kv:
             copy.start()
+
+    for copy in stage:
+        copy.wait()
+
+    @pl.when(tail == 0)
+    def _():
+        send_kv(0).start()
+
+    for n in range(1, KV):
+        send_kv(n).start()
     for copy in loads:
         copy.start()
 
@@ -184,15 +228,17 @@
 
     def query_grads(n, t, score):
         grad = dot(kvin[n, 0].T, score[:, pl.ds(t * KEYS, KEYS)], 1, 0)
-        grad = (grad.T * SCALE).astype(BF16)
+        grad = (grad * SCALE).astype(BF16).T
         target, rows = (pgrad, PROWS) if t < 4 else (rgrad, RROWS)
         for i, columns in enumerate(spans(n, t)):
             target[:, columns] = grad[i * rows : (i + 1) * rows]
 
+    def value_grads(n):
+        cotangent = jnp.concatenate([rows_of(n, t, c_p, w_r) for t in range(TILES)], axis=0)
+        part[n, 1] = dot(probs[...], cotangent, 1, 0).astype(BF16)
+
     def key_grads(n, score):
         queries = jnp.concatenate([rows_of(n, t, q_p, q_r) for t in range(TILES)], axis=0)
-        cotangent = jnp.concatenate([rows_of(n, t, c_p, w_r) for t in range(TILES)], axis=0)
-        part[n, 1] = dot(probs[...], cotangent, 1, 0).astype(BF16)
         part[n, 0] = (dot(score[...], queries, 1, 0) * SCALE).astype(BF16)
 
     def send_sum(n):
@@ -200,24 +246,61 @@
         back[n] = (part[n, :, mine, :].astype(F32) + got[n].astype(F32)).astype(BF16)
         give_back(n).start()
 
+    def pass_on(n):
+        late = n >= late_from
+
+        @pl.when(jnp.logical_not(late))
+        def _():
+            exchange(n).start()
+
+        @pl.when(jnp.logical_and(late, core != chosen))
+        def _():
+            hand_over(n).start()
+
+    def combine(n):
+        hand_over(n).wait_recv()
+        final[n - LATE] = (part[n].astype(F32) + final_got[n - LATE].astype(F32)).astype(BF16)
+        for i in range(2):
+            give_last(n, i).start()
+
+    def settle_late():
+        @pl.when(lead == 0)
+        def _():
+            send_sum(LATE)
+
+        @pl.when(jnp.logical_and(lead == 1, core == chosen))
+        def _():
+            combine(LATE)
+
+    def settle_last():
+        @pl.when(core == chosen)
+        def _():
+            combine(LAST)
+
     def step(n, score, before, first=False, last=False):
         if not (first or last):
-            kv_arrived(n + 1)
+            send_kv(n + 1).wait_recv()
             forward(n + 1).start()
         forward(n).wait_recv()
         for t in range(TILES):
             if first and t == TILES // 2:
-                kv_arrived(n + 1)
+                send_kv(n + 1).wait_recv()
                 forward(n + 1).start()
             scores(n, t, score)
             if not first:
                 query_grads(n - 1, t, before)
+        value_grads(n)
         key_grads(n, score)
-        exchange(n).start()
-        if not first:
-            send_sum(n - 1)
-
-    kv_arrived(0)
+        if first:
+            exchange(n).start()
+        else:
+            pass_on(n)
+            if last:
+                settle_late()
+            else:
+                send_sum(n - 1)
+
+    send_kv(0).wait_recv()
     forward(0).start()
     step(0, score_a, score_b, first=True)
 
@@ -230,15 +313,38 @@
     step(KV - 1, score_b, score_a, last=True)
     for t in range(TILES):
         query_grads(KV - 1, t, score_b)
-    send_sum(KV - 1)
+    settle_last()
 
     def finish(n, carry):
-        for copy in send_kv(n):
+        @pl.when(n >= tail)
+        def _():
+            send_kv(n).wait_send()
+
+        forward(n).wait_send()
+        late = n >= late_from
+
+        @pl.when(jnp.logical_not(late))
+        def _():
+            exchange(n).wait_send()
+            give_back(n).wait_send()
+
+        @pl.when(jnp.logical_and(late, core != chosen))
+        def _():
+            hand_over(n).wait_send()
+
+        @pl.when(jnp.logical_and(late, core == chosen))
+        def _():
+            for i in range(2):
+                give_last(n, i).wait_send()
+
+        give_back(n).wait_recv()
+        return carry
+
+
+    @pl.when(tail == 1)
+    def _():
+        for copy in first_kv:
             copy.wait_send()
-        forward(n).wait_send()
-        exchange(n).wait_send()
-        give_back(n).wait()
-        return carry
 
     lax.fori_loop(0, KV, finish, 0)
 
@@ -275,6 +381,7 @@
         in_specs=[main] * 13,
         out_specs=(vector, vector, vector),
         scratch_shapes=[
+            pltpu.VMEM((2, PROWS, KV * DIM), BF16),
             pltpu.VMEM((KV, 2, KEYS, DIM), BF16),
             pltpu.VMEM((PROWS, wide), BF16),
             pltpu.VMEM((PROWS, wide), BF16),
@@ -299,16 +406,21 @@
             pltpu.VMEM((KV, 2, KEYS, DIM), BF16),
             pltpu.VMEM((KV, 2, PROWS, DIM), BF16),
             pltpu.VMEM((KV, 2, PROWS, DIM), BF16),
+            pltpu.VMEM((2, 2, KEYS, DIM), BF16),
+            pltpu.VMEM((2, 2, KEYS, DIM), BF16),
+            pltpu.SemaphoreType.DMA((2,)),
+            pltpu.SemaphoreType.DMA((2,)),
             pltpu.SemaphoreType.DMA((4,)),
             pltpu.SemaphoreType.DMA((7,)),
-            pltpu.SemaphoreType.DMA((2, KV)),
-            pltpu.SemaphoreType.DMA((2, KV)),
-            pltpu.SemaphoreType.DMA((KV,)),
-            pltpu.SemaphoreType.DMA((KV,)),
-            pltpu.SemaphoreType.DMA((KV,)),
-            pltpu.SemaphoreType.DMA((KV,)),
-            pltpu.SemaphoreType.DMA((KV,)),
-            pltpu.SemaphoreType.DMA((KV,)),
+            pltpu.SemaphoreType.DMA((KV,)),
+            pltpu.SemaphoreType.DMA((KV,)),
+            pltpu.SemaphoreType.DMA((KV,)),
+            pltpu.SemaphoreType.DMA((KV,)),
+            pltpu.SemaphoreType.DMA((KV,)),
+            pltpu.SemaphoreType.DMA((KV,)),
+            pltpu.SemaphoreType.DMA((KV,)),
+            pltpu.SemaphoreType.DMA((KV,)),
+            pltpu.SemaphoreType.DMA((2, 2)),
         ],
         compiler_params=pltpu.CompilerParams(
             collective_id=0, has_side_effects=True, vmem_limit_bytes=28 * 2**20

time: 33.5 us -> 32.6 us (0.973)
  the two profiles are of different devices: /device:TPU:1 before, /device:TPU:126 now
where the time goes in v3:
time: 32.6 us; the launch traced here: 32.5 us
  Pallas kernels  31.9 us (98%)
  between operations  0.64 us (2%)
    pallas_call x1, Pallas kernels, body(): pl.pallas_call(kernel, out_shape=(pltpu.VMEM((RROWS, wide), BF16), pltpu....  30 us
    pallas_call x1, Pallas kernels, body(): pl.pallas_call(write_out, out_shape=(jax.ShapeDtypeStruct((RROWS, wide),...  1.86 us

profile of v3, /device:TPU:126, one launch (start us, length us, event | category | flops | bytes accessed | tf_op | source)
XLA Modules:
  0.0 32.5 jit_solution(14933970857759835685)
XLA Ops:
  0.6 30.0 %prefix_backward.1 = (bf16[64,8192]{1,0:T(8,128)(2,1)S(1)}, bf16[128,8192]{1,0:T(8,128)(2,1)S(1)}, bf16[2,128,1024]{2,1,0:T(8,128)(2,1)S(1)}) custom-call(bf16[128,1024]{1,0:T(8,128)(2,1)} %pk.1, bf16[128,1024]{1,0:T(8,128)(2,1)} %pv.1, s32[128]{0:T(128)} %offsets.1, bf16[128,8192]{1,0:T(8,128)(2,1)} %pq.1, bf16[128,8192]{1,0:T(8,128)(2,1)} %pc.1, ...), custom_call_target="tpu_custom_call" | custom-call | tf_op jit(solution)/shard_map/prefix_backward/pallas_call | solution.py:374
  30.6 1.9 %write_out.1 = (bf16[64,8192]{1,0:T(8,128)(2,1)}, bf16[128,8192]{1,0:T(8,128)(2,1)}, bf16[128,1024]{1,0:T(8,128)(2,1)}, bf16[128,1024]{1,0:T(8,128)(2,1)}) custom-call(bf16[64,8192]{1,0:T(8,128)(2,1)S(1)} %get-tuple-element.7.rgrad, bf16[128,8192]{1,0:T(8,128)(2,1)S(1)} %get-tuple-element.8.pgrad, bf16[2,128,1024]{2,1,0:T(8,128)(2,1)S(1)} %get-tuple-element.9.kvgrad), custom_call_target="tpu_custom_call" | custom-call | tf_op jit(solution)/shard_map/write_out/pallas_call | solution.py:431

commit v4 on v3

--- a/solution.py
+++ b/solution.py
@@ -287,9 +287,10 @@
                 send_kv(n + 1).wait_recv()
                 forward(n + 1).start()
             scores(n, t, score)
-            if not first:
+        value_grads(n)
+        if not first:
+            for t in range(TILES):
                 query_grads(n - 1, t, before)
-        value_grads(n)
         key_grads(n, score)
         if first:
             exchange(n).start()

time: 32.6 us -> 32.6 us (level)
  no operation moved by 1% of the time
where the time goes in v4:
time: 32.6 us; the launch traced here: 32.5 us
  Pallas kernels  31.8 us (98%)
  between operations  0.64 us (2%)
    pallas_call x1, Pallas kernels, body(): pl.pallas_call(kernel, out_shape=(pltpu.VMEM((RROWS, wide), BF16), pltpu....  30 us
    pallas_call x1, Pallas kernels, body(): pl.pallas_call(write_out, out_shape=(jax.ShapeDtypeStruct((RROWS, wide),...  1.86 us

profile of v4, /device:TPU:126, one launch (start us, length us, event | category | flops | bytes accessed | tf_op | source)
XLA Modules:
  0.0 32.5 jit_solution(5017050865146837812)
XLA Ops:
  0.6 30.0 %prefix_backward.1 = (bf16[64,8192]{1,0:T(8,128)(2,1)S(1)}, bf16[128,8192]{1,0:T(8,128)(2,1)S(1)}, bf16[2,128,1024]{2,1,0:T(8,128)(2,1)S(1)}) custom-call(bf16[128,1024]{1,0:T(8,128)(2,1)} %pk.1, bf16[128,1024]{1,0:T(8,128)(2,1)} %pv.1, s32[128]{0:T(128)} %offsets.1, bf16[128,8192]{1,0:T(8,128)(2,1)} %pq.1, bf16[128,8192]{1,0:T(8,128)(2,1)} %pc.1, ...), custom_call_target="tpu_custom_call" | custom-call | tf_op jit(solution)/shard_map/prefix_backward/pallas_call | solution.py:375
  30.6 1.9 %write_out.1 = (bf16[64,8192]{1,0:T(8,128)(2,1)}, bf16[128,8192]{1,0:T(8,128)(2,1)}, bf16[128,1024]{1,0:T(8,128)(2,1)}, bf16[128,1024]{1,0:T(8,128)(2,1)}) custom-call(bf16[64,8192]{1,0:T(8,128)(2,1)S(1)} %get-tuple-element.7.rgrad, bf16[128,8192]{1,0:T(8,128)(2,1)S(1)} %get-tuple-element.8.pgrad, bf16[2,128,1024]{2,1,0:T(8,128)(2,1)S(1)} %get-tuple-element.9.kvgrad), custom_call_target="tpu_custom_call" | custom-call | tf_op jit(solution)/shard_map/write_out/pallas_call | solution.py:432

commit v5 on v4

--- a/solution.py
+++ b/solution.py
@@ -41,15 +41,8 @@
     count = lax.axis_size("ctx")
     me = lax.axis_index("ctx")
     core = lax.axis_index("rsp")
-    right = lax.rem(me + 1, count)
     left = lax.rem(me + count - 1, count)
     other = 1 - core
-    lead = (count - 1 - me) // (count - 1)
-    tail = me // (count - 1)
-    chosen = 1 - lead
-    late_from = KV - 1 - lead
-    mine = pl.ds(pl.multiple_of(core * PROWS, PROWS), PROWS)
-    theirs = pl.ds(pl.multiple_of(other * PROWS, PROWS), PROWS)
 
     barrier = pltpu.get_barrier_semaphore()
     for device in ((left, core), (me, other)):
@@ -68,6 +61,14 @@
         pltpu.make_async_copy(source, target, load_sem.at[i])
         for i, (source, target) in enumerate(((rc, c_r), (pq, q_p), (pc, c_p), (rq, q_r)))
     ]
+    right = lax.rem(me + 1, count)
+    lead = (count - 1 - me) // (count - 1)
+    tail = me // (count - 1)
+    chosen = 1 - lead
+    late_from = KV - 1 - lead
+    mine = pl.ds(pl.multiple_of(core * PROWS, PROWS), PROWS)
+    theirs = pl.ds(pl.multiple_of(other * PROWS, PROWS), PROWS)
+
     stage = [pltpu.make_async_copy(source, kvsrc.at[i], stage_sem.at[i]) for i, source in enumerate((pk, pv))]
     for copy in stage + small:
         copy.start()

time: 32.6 us -> 32.6 us (level)
  no operation moved by 1% of the time
where the time goes in v5:
time: 32.6 us; the launch traced here: 32.5 us
  Pallas kernels  31.8 us (98%)
  between operations  0.64 us (2%)
    pallas_call x1, Pallas kernels, body(): pl.pallas_call(kernel, out_shape=(pltpu.VMEM((RROWS, wide), BF16), pltpu....  29.9 us
    pallas_call x1, Pallas kernels, body(): pl.pallas_call(write_out, out_shape=(jax.ShapeDtypeStruct((RROWS, wide),...  1.86 us

profile of v5, /device:TPU:126, one launch (start us, length us, event | category | flops | bytes accessed | tf_op | source)
XLA Modules:
  0.0 32.5 jit_solution(12474854065087350613)
XLA Ops:
  0.6 29.9 %prefix_backward.1 = (bf16[64,8192]{1,0:T(8,128)(2,1)S(1)}, bf16[128,8192]{1,0:T(8,128)(2,1)S(1)}, bf16[2,128,1024]{2,1,0:T(8,128)(2,1)S(1)}) custom-call(bf16[128,1024]{1,0:T(8,128)(2,1)} %pk.1, bf16[128,1024]{1,0:T(8,128)(2,1)} %pv.1, s32[128]{0:T(128)} %offsets.1, bf16[128,8192]{1,0:T(8,128)(2,1)} %pq.1, bf16[128,8192]{1,0:T(8,128)(2,1)} %pc.1, ...), custom_call_target="tpu_custom_call" | custom-call | tf_op jit(solution)/shard_map/prefix_backward/pallas_call | solution.py:376
  30.6 1.9 %write_out.1 = (bf16[64,8192]{1,0:T(8,128)(2,1)}, bf16[128,8192]{1,0:T(8,128)(2,1)}, bf16[128,1024]{1,0:T(8,128)(2,1)}, bf16[128,1024]{1,0:T(8,128)(2,1)}) custom-call(bf16[64,8192]{1,0:T(8,128)(2,1)S(1)} %get-tuple-element.7.rgrad, bf16[128,8192]{1,0:T(8,128)(2,1)S(1)} %get-tuple-element.8.pgrad, bf16[2,128,1024]{2,1,0:T(8,128)(2,1)S(1)} %get-tuple-element.9.kvgrad), custom_call_target="tpu_custom_call" | custom-call | tf_op jit(solution)/shard_map/write_out/pallas_call | solution.py:433
